TPU v7x, 256 devices: a whole 4x4x8 slice. The times are simulated.
256 devices in a mesh: coil: 32 (over z_hi, x, core), sect: 8 (over y, z_lo).
Axes of the slice: x: 4, y: 4, z: 8 (z_hi: 4, z_lo: 2; z = z_hi * 2 + z_lo), core: 2. Of those that a mesh axis runs over, the one named last changes fastest.
Arguments:
- measured: float32 [256, 32, 16, 2, 192], P(None, 'coil', 'sect'), may hold values from -6 to 6
- coil_maps: float32 [256, 32, 16, 2, 192], P(None, 'coil', 'sect'), may hold values from -0.75 to 0.75
- sampling: int32 [16, 192], P('sect'), may hold values 0 or 1
- conv_first: bfloat16 [64, 54], replicated, may hold values from -0.875 to 0.875
- bias_first: float32 [64], replicated, may hold values from -3 to 3
- conv_second: bfloat16 [54, 64], replicated, may hold values from -0.15625 to 0.15625
- bias_second: float32 [2], replicated, may hold values from -1.5 to 1.5
Outputs:
- recon: float32 [256, 16, 2, 192], P('coil', 'sect')
Inputs may be any that keep to these rules, and one draw needn't show every extreme that they name: sampling[s, l] is 1 where phase-encoding column l of slice s was measured, else 0.
All inputs are finite; a program needn't handle non-finite values. No bound on the sum of `sampling` on one device may be relied on, other than what follows from the above.
Results may differ from a plain program's by a relative error of at most 0.0029.
Values may be sent and summed in bfloat16 or wider, within the bound.
A program may use at most 64 MiB of HBM per device.

v0:
```python
import math

import jax
import jax.numpy as jnp
from jax import lax
from jax.sharding import PartitionSpec as P

ITERS = 2


step_size = 0.5
highest = lax.Precision.HIGHEST


def with_halo(x, sides, width):
    for axis, dim in sides:
        count, length = (lax.axis_size(axis), x.shape[dim])
        up = [(i, (i + 1) % count) for i in range(count - 1)]
        down = [(j, i) for i, j in up]
        last = lax.slice_in_dim(x, length - width, length, axis=dim)
        leading = lax.slice_in_dim(x, 0, width, axis=dim)
        before = lax.ppermute(last, axis, up)
        after = lax.ppermute(leading, axis, down)
        x = jnp.concatenate([before, x, after], axis=dim)
    return x


def dft_tables(length):
    index = jnp.arange(length, dtype=jnp.int32)
    phase = index[:, None] * index[None, :] % length
    angle = phase.astype(jnp.float32) * (2.0 * math.pi / length)
    factor = 1.0 / math.sqrt(length)
    return (jnp.cos(angle) * factor, jnp.sin(angle) * factor)


def along_columns(real_part, imag_part, column_pair, sign):
    stacked = jnp.stack([real_part, imag_part])
    product = jnp.dot(stacked, column_pair, precision=highest)
    breadth = column_pair.shape[0]
    out_real = product[0, ..., :breadth] - sign * product[1, ..., breadth:]
    out_imag = product[1, ..., :breadth] + sign * product[0, ..., breadth:]
    return (out_real, out_imag)


def stack_taps(padded, out_rows, out_slices, breadth):
    windows = []
    for first in range(3):
        for second in range(3):
            for third in range(3):
                windows.append(
                    padded[
                        first : first + out_rows,
                        second : second + out_slices,
                        :,
                        third : third + breadth,
                    ]
                )
    return jnp.concatenate(windows, axis=2)


def tap_sum(taps, out_rows, out_slices, breadth):
    result = jnp.zeros((out_rows, out_slices, 2, breadth), jnp.float32)
    position = 0
    for first in range(3):
        for second in range(3):
            for third in range(3):
                result = (
                    result
                    + taps[
                        first : first + out_rows,
                        second : second + out_slices,
                        2 * position : 2 * position + 2,
                        third : third + breadth,
                    ]
                )
                position = position + 1
    return result


def per_device(measured, coil_maps, sampling, conv_first, bias_first, conv_second, bias_second):
    height = coil_maps.shape[0]
    slices_here = coil_maps.shape[2]
    breadth = coil_maps.shape[4]
    rows_here = height // lax.axis_size("coil")
    row_cosine, row_sine = dft_tables(height)
    column_cosine, column_sine = dft_tables(breadth)
    column_pair = jnp.concatenate([column_cosine, column_sine], axis=1)
    weights = sampling.astype(jnp.float32)[None, None, :, None, :]
    margin = 1

    def prepare(resid):
        spread_real, spread_imag = along_columns(
            resid[:, :, :, 0, :], resid[:, :, :, 1, :], column_pair, 1.0
        )
        return jnp.stack([spread_real, spread_imag], axis=3)

    def coil_reduce(spread):
        tables = jnp.stack([row_cosine, row_sine])
        mixed = jnp.tensordot(tables, spread, axes=((2,), (0,)), precision=highest)
        inverse_real = mixed[0, :, :, :, 0, :] - mixed[1, :, :, :, 1, :]
        inverse_imag = mixed[0, :, :, :, 1, :] + mixed[1, :, :, :, 0, :]
        maps_real = coil_maps[:, :, :, 0, :]
        maps_imag = coil_maps[:, :, :, 1, :]
        total_real = jnp.sum(maps_real * inverse_real + maps_imag * inverse_imag, axis=1)
        total_imag = jnp.sum(maps_real * inverse_imag - maps_imag * inverse_real, axis=1)
        summed_rows = lax.psum_scatter(
            jnp.stack([total_real, total_imag], axis=2), "coil", scatter_dimension=0, tiled=True
        )
        return (summed_rows, None)

    image, full_image = coil_reduce(prepare(weights * measured))
    for turn in range(ITERS):
        portion = lax.all_gather(image, "coil", axis=0, tiled=True)
        image_real = portion[:, None, :, 0, :]
        image_imag = portion[:, None, :, 1, :]
        product_real = coil_maps[:, :, :, 0, :] * image_real - coil_maps[:, :, :, 1, :] * image_imag
        product_imag = coil_maps[:, :, :, 0, :] * image_imag + coil_maps[:, :, :, 1, :] * image_real
        forward_spread_real, forward_spread_imag = along_columns(
            product_real, product_imag, column_pair, -1.0
        )
        forward_tables = jnp.stack([row_cosine, row_sine])
        forward_mixed = jnp.tensordot(
            forward_tables,
            jnp.stack([forward_spread_real, forward_spread_imag], axis=3),
            axes=((2,), (0,)),
            precision=highest,
        )
        spectrum_real = forward_mixed[0, :, :, :, 0, :] + forward_mixed[1, :, :, :, 1, :]
        spectrum_imag = forward_mixed[0, :, :, :, 1, :] - forward_mixed[1, :, :, :, 0, :]
        predicted = jnp.stack([spectrum_real, spectrum_imag], axis=3)
        summed, summed_full = coil_reduce(prepare(weights * (predicted - measured)))
        damped = image - step_size * summed
        extended = with_halo(damped.astype(jnp.bfloat16), (("coil", 0), ("sect", 1)), margin)
        out_rows = extended.shape[0] - 2
        out_slices = extended.shape[1] - 2
        padded = jnp.pad(extended, ((0, 0), (0, 0), (0, 0), (1, 1)))
        columns = stack_taps(padded, out_rows, out_slices, breadth)
        hidden = jnp.einsum(
            "oc,rscw->rsow", conv_first, columns, preferred_element_type=jnp.float32
        )
        hidden = jax.nn.relu(hidden + bias_first[None, None, :, None]).astype(jnp.bfloat16)
        hidden = with_halo(hidden, (("coil", 0), ("sect", 1)), 1)
        padded_hidden = jnp.pad(hidden, ((0, 0), (0, 0), (0, 0), (1, 1)))
        taps = jnp.einsum(
            "tc,rscw->rstw", conv_second, padded_hidden, preferred_element_type=jnp.float32
        )
        update = tap_sum(taps, rows_here, slices_here, breadth) + bias_second[None, None, :, None]
        image = damped + update
    return image


def solution(mesh):
    in_specs = (
        P(None, "coil", "sect", None, None),
        P(None, "coil", "sect", None, None),
        P("sect", None),
        P(),
        P(),
        P(),
        P(),
    )
    out_specs = P("coil", "sect", None, None)
    return jax.shard_map(
        per_device, mesh=mesh, in_specs=in_specs, out_specs=out_specs, check_vma=False
    )
```

profile of v0, /device:TPU:1, one launch (start us, length us, event | category | flops | bytes accessed | tf_op | source)
XLA Modules:
  0.0 1109.2 jit_solution(506134346250771774)
XLA Ops:
  6.5 0.8 sine_multiply_fusion.1
  7.4 1.1 sine_multiply_fusion
  8.4 0.7 convert_element_type.49
  9.1 1.2 copy_multiply_fusion
  10.4 2.0 fusion.37
  12.9 2.0 convolution_bitcast_fusion.7
  15.1 1.3 copy.184
  16.5 0.6 dynamic-slice
  17.7 290.0 %all-reduce.11.cloned.1.call-done = f32[256,2,2,192]{3,2,1,0:T(2,128)} async-done(((f32[256,2,2,192]{3,2,1,0:T(2,128)}), f32[256,2,2,192]{3,2,1,0:T(2,128)}) %all-reduce.11.cloned.1.call-update) | async-done | bytes 786448
  307.7 0.8 constant_dynamic-slice_fusion
  308.5 42.8 %all_gather.6 = f32[256,2,2,192]{3,2,1,0:T(2,128)S(1)} all-gather(f32[8,2,2,192]{3,2,1,0:T(2,128)S(1)} %constant_dynamic-slice_fusion), channel_id=1, replica_groups=mesh['coil'=32,'sect'=8] {'coil'}, dimensions={0}, use_global_device_ids=true | all-gather | bytes 811008 | tf_op jit(solution)/shard_map/all_gather | solution.py:113
  351.3 0.8 fusion.142
  353.2 2.0 fusion.40
  355.6 2.0 convolution_bitcast_fusion.6
  357.7 1.0 copy-done.2
  358.9 2.0 fusion.44
  361.3 2.0 convolution_bitcast_fusion.5
  363.5 1.3 copy.197
  364.9 287.2 %all-reduce.13.cloned.1.call-done = f32[256,2,2,192]{3,2,1,0:T(2,128)} async-done(((f32[256,2,2,192]{3,2,1,0:T(2,128)}), f32[256,2,2,192]{3,2,1,0:T(2,128)}) %all-reduce.13.cloned.1.call-update) | async-done | bytes 786448
  652.2 0.8 fusion.139
  653.0 1.9 collective-permute-start
  654.9 2.4 collective-permute-start.1
  657.3 2.5 collective-permute-done.1
  659.9 2.3 collective-permute-start.2
  662.2 11.7 %collective-permute-start.3 = (bf16[10,1,2,192]{3,2,1,0:T(2,128)(2,1)S(1)}, bf16[10,1,2,192]{3,2,1,0:T(2,128)(2,1)S(1)}, u32[]{:S(2)}, u32[]{:S(2)}) collective-permute-start(bf16[10,1,2,192]{3,2,1,0:T(2,128)(2,1)S(1)} %get-tuple-element.94), channel_id=1, source_target_pairs={{1,0},{2,1},{3,2},{4,3},{5,4},{6,5},{7,6},{9,8},{10,9},{11,10},{12... | collective-permute-start | bytes 23048 | tf_op jit(solution)/shard_map/ppermute | solution.py:23
  674.5 0.7 concatenate.72
  675.6 2.2 collective-permute-start.4
  677.8 2.1 collective-permute-start.5
  680.0 3.5 collective-permute-done.5
  683.6 4.5 collective-permute-start.6
  688.2 1.3 collective-permute-start.7
  689.5 4.4 collective-permute-done.6
  693.9 9.9 collective-permute-done.7
  703.8 1.0 convolution_bitcast_fusion.1
  704.8 1.5 fusion.114
  706.2 0.6 copy-done.3
  706.9 47.1 %all_gather.7 = f32[256,2,2,192]{3,2,1,0:T(2,128)S(1)} all-gather(f32[8,2,2,192]{3,2,1,0:T(2,128)S(1)} %fusion.114), channel_id=1, replica_groups=mesh['coil'=32,'sect'=8] {'coil'}, dimensions={0}, use_global_device_ids=true | all-gather | bytes 811008 | tf_op jit(solution)/shard_map/all_gather | solution.py:113
  754.0 0.8 fusion.141
  754.8 1.1 copy.234
  756.4 1.1 fusion.87
  757.5 2.0 convolution_bitcast_fusion.2
  759.8 2.0 convolution_bitcast_fusion.4
  761.9 0.6 copy-done.8
  762.7 2.0 fusion.50
  765.1 2.0 convolution_bitcast_fusion.3
  767.4 1.3 copy.207
  768.7 287.9 %all-reduce.15.cloned.1.call-done = f32[256,2,2,192]{3,2,1,0:T(2,128)} async-done(((f32[256,2,2,192]{3,2,1,0:T(2,128)}), f32[256,2,2,192]{3,2,1,0:T(2,128)}) %all-reduce.15.cloned.1.call-update) | async-done | bytes 786448
  1056.6 0.8 fusion.140
  1057.4 1.9 collective-permute-start.8
  1059.3 2.4 collective-permute-start.9
  1061.7 2.5 collective-permute-done.9
  1064.3 2.3 collective-permute-start.10
  1066.6 1.5 collective-permute-start.11
  1068.2 3.4 collective-permute-done.11
  1072.1 0.7 concatenate.81
  1073.2 3.1 collective-permute-start.12
  1076.3 1.9 collective-permute-start.13
  1078.2 3.6 collective-permute-done.13
  1082.1 4.6 collective-permute-start.14
  1086.7 1.3 collective-permute-start.15
  1088.0 4.2 collective-permute-done.14
  1092.2 7.2 collective-permute-done.15
  1099.4 1.0 convolution_bitcast_fusion
  1100.4 2.1 fusion.112
  (90 shorter events, 7.3 us)
Async XLA Ops:
  6.5 697.2 %copy-start = (bf16[54,64]{1,0:T(8,128)(2,1)S(1)}, bf16[54,64]{1,0:T(8,128)(2,1)}, u32[]{:S(2)}) copy-start(bf16[54,64]{1,0:T(8,128)(2,1)} %param.12) | copy-start | bytes 20740
  6.5 301.2 %all-reduce.11.cloned.1.call-start = ((), (), s32[]{:S(2)}) async-start(), calls=%async_computation | async-start | bytes 2097152
  9.1 348.6 %copy-start.7 = (f32[2,192]{1,0:T(2,128)}, f32[2,192]{1,0:T(2,128)S(1)}, u32[]{:S(2)}) copy-start(f32[2,192]{1,0:T(2,128)S(1)} %convert_element_type.49) | copy-start | bytes 4612
  12.9 2.0 copy-start.1
  15.1 1.4 copy-start.13
  16.4 635.8 %all-reduce.13.cloned.1.call-start = ((), (), s32[]{:S(2)}) async-start(), calls=%async_computation.1 | async-start | bytes 2097152
  357.5 1.1 copy-start.2
  364.8 310.4 %copy-start.5 = (bf16[64,54]{0,1:T(8,128)(2,1)S(1)}, bf16[64,54]{0,1:T(8,128)(2,1)}, u32[]{:S(2)}) copy-start(bf16[64,54]{0,1:T(8,128)(2,1)} %param.10) | copy-start | bytes 20740
  364.8 310.4 %copy-start.9 = (f32[64]{0:T(128)S(1)}, f32[64]{0:T(128)}, u32[]{:S(2)}) copy-start(f32[64]{0:T(128)} %param.11) | copy-start | bytes 772
  364.9 691.7 %all-reduce.15.cloned.1.call-start = ((), (), s32[]{:S(2)}) async-start(), calls=%async_computation.2 | async-start | bytes 2097152
  653.0 4.3 collective-permute-start
  654.9 4.9 collective-permute-start.1
  659.9 14.0 %collective-permute-start.2 = (bf16[10,1,2,192]{3,2,1,0:T(2,128)(2,1)S(1)}, bf16[10,1,2,192]{3,2,1,0:T(2,128)(2,1)S(1)}, u32[]{:S(2)}, u32[]{:S(2)}) collective-permute-start(bf16[10,1,2,192]{3,2,1,0:T(2,128)(2,1)S(1)} %get-tuple-element.93), channel_id=1, source_target_pairs={{0,1},{1,2},{2,3},{3,4},{4,5},{5,6},{6,7},{8,9},{9,10},{10,11},{11... | collective-permute-start | bytes 23048 | tf_op jit(solution)/shard_map/ppermute | solution.py:22
  662.2 11.7 %collective-permute-start.3 = (bf16[10,1,2,192]{3,2,1,0:T(2,128)(2,1)S(1)}, bf16[10,1,2,192]{3,2,1,0:T(2,128)(2,1)S(1)}, u32[]{:S(2)}, u32[]{:S(2)}) collective-permute-start(bf16[10,1,2,192]{3,2,1,0:T(2,128)(2,1)S(1)} %get-tuple-element.94), channel_id=1, source_target_pairs={{1,0},{2,1},{3,2},{4,3},{5,4},{6,5},{7,6},{9,8},{10,9},{11,10},{12... | collective-permute-start | bytes 23048 | tf_op jit(solution)/shard_map/ppermute | solution.py:23
  675.6 4.3 collective-permute-start.4
  677.8 5.6 collective-permute-start.5
  683.6 10.2 collective-permute-start.6
  688.2 16.6 %copy-start.11 = (f32[2]{0:T(128)S(1)}, f32[2]{0:T(128)}, u32[]{:S(2)}) copy-start(f32[2]{0:T(128)} %param.13) | copy-start | bytes 28
  688.2 15.6 %collective-permute-start.7 = (bf16[10,1,64,192]{3,2,1,0:T(8,128)(2,1)S(1)}, bf16[10,1,64,192]{3,2,1,0:T(8,128)(2,1)S(1)}, u32[]{:S(2)}, u32[]{:S(2)}) collective-permute-start(bf16[10,1,64,192]{3,2,1,0:T(8,128)(2,1)S(1)} %get-tuple-element.34), channel_id=1, source_target_pairs={{1,0},{2,1},{3,2},{4,3},{5,4},{6,5},{7,6},{9,8},{10,9},{11,10},{12... | collective-permute-start | bytes 737288 | tf_op jit(solution)/shard_map/ppermute | solution.py:23
  706.2 0.6 copy-start.3
  761.8 0.7 copy-start.8
  767.3 289.2 %copy-start.4 = (f32[8,2,2,192]{3,2,1,0:T(2,128)S(1)}, f32[8,2,2,192]{3,2,1,0:T(2,128)}, u32[]{:S(2)}) copy-start(f32[8,2,2,192]{3,2,1,0:T(2,128)} %copy-done.3) | copy-start | bytes 73732
  768.7 304.1 %copy-start.6 = (bf16[64,54]{0,1:T(8,128)(2,1)S(1)}, bf16[64,54]{0,1:T(8,128)(2,1)}, u32[]{:S(2)}) copy-start(bf16[64,54]{0,1:T(8,128)(2,1)} %param.10) | copy-start | bytes 20740
  768.7 304.1 %copy-start.10 = (f32[64]{0:T(128)S(1)}, f32[64]{0:T(128)}, u32[]{:S(2)}) copy-start(f32[64]{0:T(128)} %param.11) | copy-start | bytes 772
  1057.4 4.3 collective-permute-start.8
  1059.3 4.9 collective-permute-start.9
  1064.3 3.9 collective-permute-start.10
  1066.6 4.9 collective-permute-start.11
  1073.2 5.0 collective-permute-start.12
  1076.3 5.6 collective-permute-start.13
  1082.1 10.1 collective-permute-start.14
  1086.7 13.7 %copy-start.12 = (f32[2]{0:T(128)S(1)}, f32[2]{0:T(128)}, u32[]{:S(2)}) copy-start(f32[2]{0:T(128)} %param.13) | copy-start | bytes 28
  1086.7 12.7 %collective-permute-start.15 = (bf16[10,1,64,192]{3,2,1,0:T(8,128)(2,1)S(1)}, bf16[10,1,64,192]{3,2,1,0:T(8,128)(2,1)S(1)}, u32[]{:S(2)}, u32[]{:S(2)}) collective-permute-start(bf16[10,1,64,192]{3,2,1,0:T(8,128)(2,1)S(1)} %get-tuple-element.32), channel_id=1, source_target_pairs={{1,0},{2,1},{3,2},{4,3},{5,4},{6,5},{7,6},{9,8},{10,9},{11,10},{12... | collective-permute-start | bytes 737288 | tf_op jit(solution)/shard_map/ppermute | solution.py:23
Sparse Core Ops, SparseCore 0:
  16.5 291.1 all-reduce.10
  365.0 287.1 all-reduce.12
  768.8 287.7 all-reduce.14
where the time goes:
time: 1120 us; the launch traced here: 1110 us
  waiting for transfers between devices  906 us (81%)
  blocking collectives  90 us (8%)
  starting transfers between devices  47.5 us (4%)
  matrix products  22.5 us (2%)
  between operations  14.8 us (1%)
  other arithmetic  14.1 us (1%)
  local copies, waits for them, and re-layouts  13.9 us (1%)
    unnamed x6, waiting for transfers between devices  865 us
    all_gather x2, blocking collectives, per_device(): portion = lax.all_gather(image, 'coil', axis=0, tiled=True)  90 us
    ppermute x8, waiting for transfers between devices, with_halo(): after = lax.ppermute(leading, axis, down)  32.6 us
    ppermute x8, starting transfers between devices, with_halo(): after = lax.ppermute(leading, axis, down)  24.5 us
    ppermute x8, starting transfers between devices, with_halo(): before = lax.ppermute(last, axis, up)  22.9 us
  transfers between devices with their start and end apart: 19, of which 12 were waited for; matrix products, arithmetic and copies ran while one was open for 0% of the time, Pallas kernels for 0%

commit v1 on v0

v1 whole, which is shorter than its diff:
```python
import math

import jax
import jax.numpy as jnp
import ml_dtypes
import numpy as np
from jax import lax
from jax.experimental import pallas as pl
from jax.experimental.pallas import tpu as pltpu
from jax.sharding import PartitionSpec as P

ITERS = 2
STEP = 0.5
X_CHIPS = 4
W = 192
CH = 64
ROWS = 8
F32 = jnp.float32
BF16 = jnp.bfloat16
MESH = pl.DeviceIdType.MESH

PACKED = np.concatenate([np.arange(0, 128), np.arange(192, 320), np.arange(128, 192), np.arange(320, 384)])
OFFSETS = [(i, j) for i in (-1, 0, 1) for j in (-1, 0, 1) if (i, j) != (0, 0)]


def split_halves(table):
    high = table.astype(ml_dtypes.bfloat16)
    low = (table - high.astype(np.float64)).astype(ml_dtypes.bfloat16)
    return high, low


def dft(length):
    index = np.arange(length)
    angle = (index[:, None] * index[None, :] % length) * (2.0 * math.pi / length)
    return np.cos(angle) / math.sqrt(length), np.sin(angle) / math.sqrt(length)


def tables(height):
    cosine, sine = dft(W)
    column = np.block([[cosine, -sine], [sine, cosine]])[PACKED][:, PACKED]
    cosine, sine = dft(height)
    row = np.concatenate([cosine, sine], axis=1)
    pick_first = np.zeros((4, 54, 144), np.float32)
    pick_second = np.zeros((4, 72, 54), np.float32)
    for a in range(3):
        for b in range(3):
            for e in range(3):
                for q in range(2):
                    tap = 2 * (9 * a + 3 * b + e) + q
                    for s in range(4):
                        pick_first[s, tap, 48 * e + 16 * a + 2 * (s + b) + q] = 1.0
                        if 0 <= s - b < 2:
                            pick_second[s, 24 * a + 8 * e + 2 * (s - b) + q, tap] = 1.0
    repeat = np.tile(np.eye(CH, dtype=np.float32), (1, 4))
    as_half = lambda t: t.astype(ml_dtypes.bfloat16)
    return split_halves(column) + split_halves(row) + (as_half(pick_first), as_half(pick_second), as_half(repeat))


def dot(a, b, dims=((1,), (0,))):
    return lax.dot_general(a, b, (dims, ((), ())), preferred_element_type=F32)


def halves(value):
    high = value.astype(BF16)
    return high, (value - high.astype(F32)).astype(BF16)


def pack_rows(value):
    return jnp.concatenate([value[0:128], value[192:320], value[128:192], value[320:384]], axis=0)


def low_lanes(shape):
    return lax.broadcasted_iota(jnp.int32, shape, len(shape) - 1) < 64


def unpack(value):
    third = value[:, 256:384]
    low = low_lanes(third.shape)
    real = (value[:, 0:128], jnp.where(low, third, 0.0))
    imag = (value[:, 128:256], jnp.where(low, pltpu.roll(third, 64, 1), 0.0))
    return real, imag


def pack(real, imag):
    third = jnp.where(low_lanes(real[1].shape), real[1], pltpu.roll(imag[1], 64, 1))
    return jnp.concatenate([real[0], imag[0], third], axis=1)


def kernel(n, sections, meas_hbm, maps_hbm, th_hbm, tl_hbm, eh_hbm, el_hbm,
           samp_ref, first_ref, bias_first_ref, second_ref, bias_second_ref, pick_first_ref, pick_second_ref,
           repeat_ref, out_ref,
           meas, maps, th, tl, eh, el, masked, spread, outgoing, gathered, gathered_f, gathered_swap,
           part, got1, sum1, got2, sum2, got3, weight1, weight2, bias_full, edge_out, edge_in, grid_rows, grid_half,
           result, load_sem, maps_send, maps_recv, rs1_send, rs1_recv, rs2_send, rs2_recv, rs3_send, rs3_recv,
           edge_send, edge_recv):
    coil = lax.axis_index("coil")
    sect = lax.axis_index("sect")
    core = lax.rem(coil, 2)
    x_size = sum1.shape[2]
    z_size = sum1.shape[1]
    x = lax.rem(coil // 2, x_size)
    z = coil // (2 * x_size)

    loads = [
        pltpu.make_async_copy(src, dst, load_sem.at[i])
        for i, (src, dst) in enumerate(
            [(maps_hbm, maps), (meas_hbm, meas), (th_hbm, th), (tl_hbm, tl), (eh_hbm, eh), (el_hbm, el)]
        )
    ]
    for load in loads:
        load.start()

    barrier = pltpu.get_barrier_semaphore()

    def greet(d, carry):
        pl.semaphore_signal(barrier, inc=1, device_id=(lax.rem(coil + d, n), sect), device_id_type=MESH)
        return carry

    lax.fori_loop(1, n, greet, 0)
    for dc in (-1, 0, 1):
        for ds in (-1, 1):
            peer = (lax.rem(coil + dc + n, n), lax.rem(sect + ds + sections, sections))
            pl.semaphore_signal(barrier, inc=1, device_id=peer, device_id_type=MESH)

    loads[0].wait()
    turned = [pack_rows(maps[s]).T.reshape(n, ROWS, 384) for s in range(2)]
    outgoing[...] = jnp.concatenate(turned, axis=1).astype(BF16)
    gathered[coil] = outgoing[coil]
    pl.semaphore_wait(barrier, n - 1 + 6)

    def maps_copy(d):
        peer = lax.rem(coil + d, n)
        return pltpu.make_async_remote_copy(
            src_ref=outgoing.at[peer], dst_ref=gathered.at[coil], send_sem=maps_send.at[d], recv_sem=maps_recv.at[d],
            device_id=(peer, sect), device_id_type=MESH,
        )

    def send_maps(d, carry):
        maps_copy(d).start()
        return carry

    lax.fori_loop(1, n, send_maps, 0)

    loads[2].wait()
    loads[3].wait()
    for s in range(2):
        mask = samp_ref[s:s + 1, :].astype(F32)
        mask = jnp.concatenate([mask, jnp.zeros((1, 64), F32)], axis=1)
        tail = mask[:, 128:256]
        mask = jnp.concatenate([mask[:, 0:128], mask[:, 0:128], tail + pltpu.roll(tail, 64, 1)], axis=1)
        masked[s, 0] = (th[...].astype(F32) * mask).astype(BF16)
        masked[s, 1] = (tl[...].astype(F32) * mask).astype(BF16)

    loads[1].wait()
    loads[4].wait()
    loads[5].wait()
    copies1 = []
    for s in range(2):
        xh, xl = halves(pack_rows(meas[s]))
        column = dot(masked[s, 0], xh) + dot(masked[s, 0], xl) + dot(masked[s, 1], xh)
        zh, zl = halves(column)
        both = dot(zh, eh[...]) + dot(zl, eh[...]) + dot(zh, el[...])
        height = both.shape[1] // 2
        by_cos, by_sin = both[:, :height], both[:, height:]
        m = pack_rows(maps[s])
        terms = []
        for r0, i0, size in ((0, 128, 128), (256, 320, 64)):
            re, im = slice(r0, r0 + size), slice(i0, i0 + size)
            y_re = by_cos[re] - by_sin[im]
            y_im = by_cos[im] + by_sin[re]
            terms += [m[re] * y_re + m[im] * y_im, m[re] * y_im - m[im] * y_re]
        part[s] = jnp.concatenate(terms, axis=0).T.reshape(n // 2, 2, ROWS, 384)
        copy = pltpu.make_async_remote_copy(
            src_ref=part.at[s, :, 1 - core], dst_ref=got1.at[s], send_sem=rs1_send.at[s], recv_sem=rs1_recv.at[s],
            device_id=(coil + 1 - 2 * core, sect), device_id_type=MESH,
        )
        copy.start()
        copies1.append(copy)

    copies2 = []
    for s in range(2):
        copies1[s].wait_recv()
        sum1[s] = (part[s, :, core] + got1[s]).reshape(z_size, x_size, ROWS, 384)
        for d in range(1, x_size):
            to = lax.rem(x + d, x_size)
            copy = pltpu.make_async_remote_copy(
                src_ref=sum1.at[s, :, to], dst_ref=got2.at[s, d - 1],
                send_sem=rs2_send.at[s, d - 1], recv_sem=rs2_recv.at[s, d - 1],
                device_id=((z * x_size + to) * 2 + core, sect), device_id_type=MESH,
            )
            copy.start()
            copies2.append(copy)

    for s in range(2):
        last = ((1,), (1,))
        mh, ml = masked[s, 0], masked[s, 1]
        high, low = halves(dot(mh, mh, last) + dot(mh, ml, last) + dot(ml, mh, last))
        spread[s, 0] = high
        spread[s, 1] = low

    copies3 = []
    for s in range(2):
        total = sum1[s, :, x]
        for d in range(1, x_size):
            copies2[s * (x_size - 1) + d - 1].wait_recv()
            total = total + got2[s, d - 1]
        sum2[s] = total
        for d in range(1, z_size):
            to = lax.rem(z + d, z_size)
            copy = pltpu.make_async_remote_copy(
                src_ref=sum2.at[s, to], dst_ref=got3.at[s, d - 1],
                send_sem=rs3_send.at[s, d - 1], recv_sem=rs3_recv.at[s, d - 1],
                device_id=((to * x_size + x) * 2 + core, sect), device_id_type=MESH,
            )
            copy.start()
            copies3.append(copy)

    for s in range(4):
        weight1[64 * s:64 * s + 64] = dot(first_ref[...], pick_first_ref[s], ((0,), (0,))).astype(BF16)
    repeated = dot(second_ref[...], repeat_ref[...]).astype(BF16)
    of_slice = lax.broadcasted_iota(jnp.int32, (72, 256), 1) // 64
    second = jnp.zeros((72, 256), F32)
    for s in range(4):
        inside = jnp.logical_and(2 * sect - 1 + s >= 0, 2 * sect - 1 + s < 2 * sections)
        block = dot(pick_second_ref[s], repeated)
        second = second + jnp.where(jnp.logical_and(of_slice == s, inside), block, 0.0)
    weight2[...] = second.astype(BF16)
    diagonal = lax.broadcasted_iota(jnp.int32, (64, 64), 0) == lax.broadcasted_iota(jnp.int32, (64, 64), 1)
    bias_column = jnp.sum(jnp.where(diagonal, bias_first_ref[...], 0.0), axis=1, keepdims=True)
    for s in range(4):
        bias_full[64 * s:64 * s + 64] = jnp.broadcast_to(bias_column, (64, 256))
    grid_rows[...] = jnp.zeros_like(grid_rows)

    def wait_maps(d, carry):
        maps_copy(d).wait()
        return carry

    lax.fori_loop(1, n, wait_maps, 0)
    every = gathered[...].astype(F32)
    for s in range(2):
        mine = every[:, ROWS * s:ROWS * s + ROWS, :]
        gathered_f[s] = mine
        gathered_swap[s] = pltpu.roll(mine[:, :, 256:384].reshape(n * ROWS, 128), 64, 1).reshape(n, ROWS, 128)

    first_image = []
    for s in range(2):
        total = sum2[s, z]
        for d in range(1, z_size):
            copies3[s * (z_size - 1) + d - 1].wait_recv()
            total = total + got3[s, d - 1]
        first_image.append(total)

    lane = lax.broadcasted_iota(jnp.int32, (ROWS, 128), 1)
    low = lane < 64
    lanes_in = lax.broadcasted_iota(jnp.int32, (72, 256), 1) < W
    row_of_8 = lax.broadcasted_iota(jnp.int32, (ROWS, 256), 0)
    bias_rows = jnp.where(lax.rem(row_of_8, 2) == 0, bias_second_ref[0], bias_second_ref[1])
    image = first_image
    edge_copies = []
    for turn in range(ITERS):
        damped = []
        for s in range(2):
            v = image[s]
            va, vb, vc = v[:, 0:128], v[:, 128:256], v[:, 256:384]
            turned_c = pltpu.roll(vc, 64, 1)
            v_re = jnp.where(low, vc, turned_c)[None]
            v_im = jnp.where(low, -turned_c, vc)[None]
            ma, mb, mc = gathered_f[s, :, :, 0:128], gathered_f[s, :, :, 128:256], gathered_f[s, :, :, 256:384]
            ms = gathered_swap[s]
            va, vb = va[None], vb[None]
            pieces = [ma * va - mb * vb, ma * vb + mb * va, mc * v_re + ms * v_im]
            product = jnp.concatenate([p.reshape(n * ROWS, 128) for p in pieces], axis=1).astype(BF16)
            back = (dot(product, spread[s, 0]) + dot(product, spread[s, 1])).reshape(n, ROWS, 384)
            qa, qb, qc = back[:, :, 0:128], back[:, :, 128:256], back[:, :, 256:384]
            oa = jnp.sum(ma * qa + mb * qb, axis=0)
            ob = jnp.sum(ma * qb - mb * qa, axis=0)
            same = jnp.sum(mc * qc, axis=0)
            cross = jnp.sum(ms * qc, axis=0)
            oc = jnp.where(low, same + pltpu.roll(same, 64, 1), cross - pltpu.roll(cross, 64, 1))
            summed = jnp.concatenate([oa, ob, oc], axis=1)
            damped.append(v - STEP * (summed - first_image[s]))

        edge_out[turn] = jnp.concatenate(damped, axis=0).astype(BF16)
        copies = []
        for i, (dc, ds) in enumerate(OFFSETS):
            peer = (lax.rem(coil + dc + n, n), lax.rem(sect + ds + sections, sections))
            copy = pltpu.make_async_remote_copy(
                src_ref=edge_out.at[turn], dst_ref=edge_in.at[turn, i],
                send_sem=edge_send.at[turn, i], recv_sem=edge_recv.at[turn, i],
                device_id=peer, device_id_type=MESH,
            )
            copy.start()
            copies.append(copy)
        edge_copies += copies

        for dc, ds in [(0, 0)] + [(-i, -j) for i, j in OFFSETS]:
            if (dc, ds) == (0, 0):
                blocks = damped
            else:
                i = OFFSETS.index((-dc, -ds))
                copies[i].wait_recv()
                inside = jnp.logical_and(
                    jnp.logical_and(coil + dc >= 0, coil + dc < n),
                    jnp.logical_and(sect + ds >= 0, sect + ds < sections),
                )
                block = jnp.where(inside, edge_in[turn, i].astype(F32), 0.0)
                blocks = [block[0:ROWS], block[ROWS:2 * ROWS]]
            for s in range(2):
                for q, value in enumerate(unpack(blocks[s])):
                    k = 2 * (2 + 2 * ds + s) + q
                    for t in range(2):
                        if dc == 0:
                            grid_rows[t, pl.ds(32 + k, ROWS, stride=16), :] = value[t]
                        elif dc < 0:
                            grid_rows[t, k:k + 1, :] = value[t][ROWS - 2:ROWS - 1]
                            grid_rows[t, 16 + k:17 + k, :] = value[t][ROWS - 1:ROWS]
                        else:
                            grid_rows[t, 160 + k:161 + k, :] = value[t][0:1]
                            grid_rows[t, 176 + k:177 + k, :] = value[t][1:2]
        rows = jnp.concatenate([grid_rows[0], grid_rows[1]], axis=1)
        grid_half[0] = pltpu.roll(rows, 1, 1).astype(BF16)
        grid_half[1] = rows.astype(BF16)
        grid_half[2] = pltpu.roll(rows, 255, 1).astype(BF16)

        sums = [None] * ROWS
        for r in range(ROWS + 2):
            taps = jnp.concatenate([grid_half[e, 16 * r:16 * r + 48, :] for e in range(3)], axis=0)
            hidden = jnp.maximum(dot(weight1[...], taps) + bias_full[...], 0.0).astype(BF16)
            spots = jnp.where(lanes_in, dot(weight2[...], hidden), 0.0)
            if r == 0:
                spots = jnp.where(coil > 0, spots, 0.0)
            if r == ROWS + 1:
                spots = jnp.where(coil < n - 1, spots, 0.0)
            for a in range(3):
                if 0 <= r - a < ROWS:
                    piece = spots[24 * a:24 * a + 24]
                    sums[r - a] = piece if sums[r - a] is None else sums[r - a] + piece
        for r in range(ROWS):
            update = pltpu.roll(sums[r][0:8], 1, 1) + sums[r][8:16] + pltpu.roll(sums[r][16:24], 255, 1) + bias_rows
            for t in range(2):
                result[t, 8 * r:8 * r + 8, :] = update[:, 128 * t:128 * t + 128]

        image = []
        for s in range(2):
            update = [[result[t, pl.ds(2 * s + q, ROWS, stride=8), :] for t in range(2)] for q in range(2)]
            if turn < ITERS - 1:
                image.append(damped[s] + pack(*update))
            else:
                for q, value in enumerate(unpack(damped[s])):
                    for t in range(2):
                        result[t, pl.ds(2 * s + q, ROWS, stride=8), :] = value[t] + update[q][t]

    out_ref[:, 0:128] = result[0]
    out_ref[:, 128:256] = result[1]
    for copy in copies1 + copies2 + copies3 + edge_copies:
        copy.wait_send()


def per_device(n, sections, measured, coil_maps, sampling, conv_first, bias_first, conv_second, bias_second):
    height = measured.shape[0]
    by_columns = lambda t: t.transpose(1, 2, 3, 4, 0).reshape(2, 2 * W, height)
    consts = [jnp.asarray(t) for t in tables(height)]
    chips = n // 2
    x_size = min(X_CHIPS, chips // 2)
    z_size = chips // x_size
    vmem = pl.BlockSpec(memory_space=pltpu.VMEM)
    hbm = pl.BlockSpec(memory_space=pl.ANY)
    dma = pltpu.SemaphoreType.DMA
    out = pl.pallas_call(
        lambda *refs: kernel(n, sections, *refs),
        out_shape=jax.ShapeDtypeStruct((8 * ROWS, 256), F32),
        in_specs=[hbm] * 6 + [vmem] * 4 + [pl.BlockSpec(memory_space=pltpu.SMEM)] + [vmem] * 3,
        out_specs=vmem,
        scratch_shapes=[
            pltpu.VMEM((2, 384, height), F32),
            pltpu.VMEM((2, 384, height), F32),
            pltpu.VMEM((384, 384), BF16),
            pltpu.VMEM((384, 384), BF16),
            pltpu.VMEM((height, 2 * height), BF16),
            pltpu.VMEM((height, 2 * height), BF16),
            pltpu.VMEM((2, 2, 384, 384), BF16),
            pltpu.VMEM((2, 2, 384, 384), BF16),
            pltpu.VMEM((n, 2 * ROWS, 384), BF16),
            pltpu.VMEM((n, 2 * ROWS, 384), BF16),
            pltpu.VMEM((2, n, ROWS, 384), F32),
            pltpu.VMEM((2, n, ROWS, 128), F32),
            pltpu.VMEM((2, chips, 2, ROWS, 384), F32),
            pltpu.VMEM((2, chips, ROWS, 384), F32),
            pltpu.VMEM((2, z_size, x_size, ROWS, 384), F32),
            pltpu.VMEM((2, x_size - 1, z_size, ROWS, 384), F32),
            pltpu.VMEM((2, z_size, ROWS, 384), F32),
            pltpu.VMEM((2, z_size - 1, ROWS, 384), F32),
            pltpu.VMEM((256, 144), BF16),
            pltpu.VMEM((72, 256), BF16),
            pltpu.VMEM((256, 256), F32),
            pltpu.VMEM((ITERS, 2 * ROWS, 384), BF16),
            pltpu.VMEM((ITERS, 8, 2 * ROWS, 384), BF16),
            pltpu.VMEM((2, 192, 128), F32),
            pltpu.VMEM((3, 192, 256), BF16),
            pltpu.VMEM((2, 8 * ROWS, 128), F32),
            dma((6,)),
            dma((n,)),
            dma((n,)),
            dma((2,)),
            dma((2,)),
            dma((2, x_size - 1)),
            dma((2, x_size - 1)),
            dma((2, z_size - 1)),
            dma((2, z_size - 1)),
            dma((ITERS, 8)),
            dma((ITERS, 8)),
        ],
        compiler_params=pltpu.CompilerParams(
            collective_id=0, has_side_effects=True, vmem_limit_bytes=40 * 1024 * 1024
        ),
        name="reconstruct",
    )(
        by_columns(measured), by_columns(coil_maps), *consts[:4],
        sampling, conv_first.T, bias_first.reshape(1, CH), conv_second, bias_second, *consts[4:],
    )
    return out.reshape(ROWS, 8, 256)[:, :4, :W].reshape(ROWS, 2, 2, W)


def solution(mesh):
    n, sections = mesh.shape["coil"], mesh.shape["sect"]
    split = P(None, "coil", "sect", None, None)
    return jax.shard_map(
        lambda *args: per_device(n, sections, *args),
        mesh=mesh,
        in_specs=(split, split, P("sect", None), P(), P(), P(), P()),
        out_specs=P("coil", "sect", None, None),
        check_vma=False,
    )
```

time: 1120 us -> 60 us (0.05)
  waiting for transfers between devices: 906 us -> 0 us
  blocking collectives: 90 us -> 0 us
  Pallas kernels: 0 us -> 48.1 us
  starting transfers between devices: 47.5 us -> 0 us
  matrix products: 22.5 us -> 0 us
  between operations: 14.8 us -> 0.03 us
  other arithmetic: 14.1 us -> 0 us
    unnamed x6 -> x0, waiting for transfers between devices: 865 us -> none
    all_gather x2 -> x0, blocking collectives: 90 us -> none  [per_device(): portion = lax.all_gather(image, 'coil', axis=0, tiled=True)]
    pallas_call x0 -> x1, Pallas kernels: none -> 48.1 us  [per_device(): pl.pallas_call(lambda *refs: kernel(n, sections, *refs), out_shape=jax.Sh...]
    ppermute x16 -> x0, starting transfers between devices: 47.4 us -> none  [the longest x8 24.5 us: with_halo(): after = lax.ppermute(leading, axis, down)]
    ppermute x16 -> x0, waiting for transfers between devices: 41.2 us -> none  [the longest x8 32.6 us: with_halo(): after = lax.ppermute(leading, axis, down)]
    dot_general x14 -> x0, matrix products: 22.5 us -> none  [the longest x5 10 us: along_columns(): product = jnp.dot(stacked, column_pair, precision=highest)]
  transfers between devices with their start and end apart: 19 -> 0, of which waited for: 12 -> 0; matrix products, arithmetic and copies ran while one was open for 0% -> 0% of each run, Pallas kernels for 0% -> 0%
where the time goes in v1:
time: 60 us; the launch traced here: 59.5 us
  Pallas kernels  48.1 us (80%)
  local copies, waits for them, and re-layouts  11.4 us (19%)
    pallas_call x1, Pallas kernels, per_device(): pl.pallas_call(lambda *refs: kernel(n, sections, *refs), out_shape=jax.Sh...  48.1 us
    unnamed x28, local copies, waits for them, and re-layouts  10.7 us

profile of v1, /device:TPU:1, one launch (start us, length us, event | category | flops | bytes accessed | tf_op | source)
XLA Modules:
  0.0 59.5 jit_solution(11473201172424838888)
XLA Ops:
  0.0 0.0 copy-start.11
  0.0 0.0 copy-start.12
  0.0 0.0 copy-start.13
  0.0 0.7 %copy-done.11 = s32[2,192]{1,0:T(2,128)S(1)} copy-done((s32[2,192]{1,0:T(2,128)S(1)}, s32[2,192]{1,0:T(2,128)}, u32[]{:S(2)}) %copy-start.11) | copy-done | bytes 1560
  0.7 0.0 copy-done.12
  0.7 0.0 copy-done.13
  0.7 0.0 copy-start
  0.7 1.1 %copy-done = f32[256,1,2,2,192]{0,4,3,2,1:T(8,128)S(1)} copy-done((f32[256,1,2,2,192]{0,4,3,2,1:T(8,128)S(1)}, f32[256,1,2,2,192]{0,4,3,2,1:T(8,128)}, u32[]{:S(2)}) %copy-start) | copy-done | bytes 786456
  1.8 0.0 copy-start.1
  1.8 1.1 %copy-done.1 = f32[256,1,2,2,192]{0,4,3,2,1:T(8,128)S(1)} copy-done((f32[256,1,2,2,192]{0,4,3,2,1:T(8,128)S(1)}, f32[256,1,2,2,192]{0,4,3,2,1:T(8,128)}, u32[]{:S(2)}) %copy-start.1) | copy-done | bytes 786456
  3.0 0.0 copy-start.2
  3.0 1.0 %copy-done.2 = bf16[384,384]{1,0:T(8,128)(2,1)S(1)} copy-done((bf16[384,384]{1,0:T(8,128)(2,1)S(1)}, bf16[384,384]{1,0:T(8,128)(2,1)}, u32[]{:S(2)}) %copy-start.2) | copy-done | bytes 294936
  3.9 0.0 copy-start.3
  3.9 1.0 %copy-done.3 = bf16[384,384]{1,0:T(8,128)(2,1)S(1)} copy-done((bf16[384,384]{1,0:T(8,128)(2,1)S(1)}, bf16[384,384]{1,0:T(8,128)(2,1)}, u32[]{:S(2)}) %copy-start.3) | copy-done | bytes 294936
  4.9 0.0 copy-start.4
  4.9 0.9 %copy-done.4 = bf16[256,512]{1,0:T(8,128)(2,1)S(1)} copy-done((bf16[256,512]{1,0:T(8,128)(2,1)S(1)}, bf16[256,512]{1,0:T(8,128)(2,1)}, u32[]{:S(2)}) %copy-start.4) | copy-done | bytes 262168
  5.8 0.0 copy-start.5
  5.8 0.9 %copy-done.5 = bf16[256,512]{1,0:T(8,128)(2,1)S(1)} copy-done((bf16[256,512]{1,0:T(8,128)(2,1)S(1)}, bf16[256,512]{1,0:T(8,128)(2,1)}, u32[]{:S(2)}) %copy-start.5) | copy-done | bytes 262168
  6.8 0.0 copy-start.6
  6.8 0.9 %copy-done.6 = bf16[4,54,144]{2,1,0:T(8,128)(2,1)S(1)} copy-done((bf16[4,54,144]{2,1,0:T(8,128)(2,1)S(1)}, bf16[4,54,144]{2,1,0:T(8,128)(2,1)}, u32[]{:S(2)}) %copy-start.6) | copy-done | bytes 62232
  7.7 0.0 copy-start.7
  7.7 0.9 %copy-done.7 = bf16[4,72,54]{2,1,0:T(8,128)(2,1)S(1)} copy-done((bf16[4,72,54]{2,1,0:T(8,128)(2,1)S(1)}, bf16[4,72,54]{2,1,0:T(8,128)(2,1)}, u32[]{:S(2)}) %copy-start.7) | copy-done | bytes 31128
  8.6 0.0 copy-start.8
  8.6 0.8 %copy-done.8 = bf16[64,256]{1,0:T(8,128)(2,1)S(1)} copy-done((bf16[64,256]{1,0:T(8,128)(2,1)S(1)}, bf16[64,256]{1,0:T(8,128)(2,1)}, u32[]{:S(2)}) %copy-start.8) | copy-done | bytes 32792
  9.3 0.0 copy-start.9
  9.3 0.7 %copy-done.9 = bf16[64,54]{0,1:T(8,128)(2,1)S(1)} copy-done((bf16[64,54]{0,1:T(8,128)(2,1)S(1)}, bf16[64,54]{0,1:T(8,128)(2,1)}, u32[]{:S(2)}) %copy-start.9) | copy-done | bytes 6936
  10.0 0.0 copy-start.10
  10.0 0.7 %copy-done.10 = bf16[54,64]{1,0:T(8,128)(2,1)S(1)} copy-done((bf16[54,64]{1,0:T(8,128)(2,1)S(1)}, bf16[54,64]{1,0:T(8,128)(2,1)}, u32[]{:S(2)}) %copy-start.10) | copy-done | bytes 6936
  10.7 48.1 %reconstruct.1 = f32[64,256]{1,0:T(8,128)S(1)} custom-call(f32[2,384,256]{2,1,0:T(8,128)S(1)} %bitcast.9, f32[2,384,256]{2,1,0:T(8,128)S(1)} %bitcast.10, bf16[384,384]{1,0:T(8,128)(2,1)S(1)} %copy-done.3, bf16[384,384]{1,0:T(8,128)(2,1)S(1)} %copy-done.2, bf16[256,512]{1,0:T(8,128)(2,1)S(1)} %copy-done.5, bf16[256,512]{1,0:T(8,128)(2,1)S(1)} %copy-done.4, ...), custom_call_target="tpu_custom_call" | custom-call | tf_op jit(solution)/shard_map/reconstruct/pallas_call | solution.py:369
  58.9 0.6 %reshape.19 = f32[8,2,2,192]{3,2,1,0:T(2,128)} reshape(f32[8,4,192]{2,1,0:T(4,128)S(1)} %slice.4) | data formatting | bytes 49152 | tf_op jit(solution)/shard_map/reshape | solution.py:421
  (1 shorter events, 0.0 us)
Async XLA Ops:
  0.0 0.7 %copy-start.11 = (s32[2,192]{1,0:T(2,128)S(1)}, s32[2,192]{1,0:T(2,128)}, u32[]{:S(2)}) copy-start(s32[2,192]{1,0:T(2,128)} %refs_6_.1) | copy-start | bytes 4612
  0.0 0.7 %copy-start.12 = (f32[64]{0:T(128)S(1)}, f32[64]{0:T(128)}, u32[]{:S(2)}) copy-start(f32[64]{0:T(128)} %param.18) | copy-start | bytes 772
  0.0 0.7 %copy-start.13 = (f32[2]{0:T(128)S(1)}, f32[2]{0:T(128)}, u32[]{:S(2)}) copy-start(f32[2]{0:T(128)} %refs_10_.1) | copy-start | bytes 28
  0.7 1.1 %copy-start = (f32[256,1,2,2,192]{0,4,3,2,1:T(8,128)S(1)}, f32[256,1,2,2,192]{0,4,3,2,1:T(8,128)}, u32[]{:S(2)}) copy-start(f32[256,1,2,2,192]{0,4,3,2,1:T(8,128)} %param.14) | copy-start | bytes 2359300
  1.8 1.1 %copy-start.1 = (f32[256,1,2,2,192]{0,4,3,2,1:T(8,128)S(1)}, f32[256,1,2,2,192]{0,4,3,2,1:T(8,128)}, u32[]{:S(2)}) copy-start(f32[256,1,2,2,192]{0,4,3,2,1:T(8,128)} %param.15) | copy-start | bytes 2359300
  3.0 1.0 %copy-start.2 = (bf16[384,384]{1,0:T(8,128)(2,1)S(1)}, bf16[384,384]{1,0:T(8,128)(2,1)}, u32[]{:S(2)}) copy-start(bf16[384,384]{1,0:T(8,128)(2,1)} %constant.15.clone.refs_3_) | copy-start | bytes 884740
  3.9 1.0 %copy-start.3 = (bf16[384,384]{1,0:T(8,128)(2,1)S(1)}, bf16[384,384]{1,0:T(8,128)(2,1)}, u32[]{:S(2)}) copy-start(bf16[384,384]{1,0:T(8,128)(2,1)} %constant.14.clone.refs_2_) | copy-start | bytes 884740
  4.9 0.9 %copy-start.4 = (bf16[256,512]{1,0:T(8,128)(2,1)S(1)}, bf16[256,512]{1,0:T(8,128)(2,1)}, u32[]{:S(2)}) copy-start(bf16[256,512]{1,0:T(8,128)(2,1)} %constant.17.clone.refs_5_) | copy-start | bytes 786436
  5.8 0.9 %copy-start.5 = (bf16[256,512]{1,0:T(8,128)(2,1)S(1)}, bf16[256,512]{1,0:T(8,128)(2,1)}, u32[]{:S(2)}) copy-start(bf16[256,512]{1,0:T(8,128)(2,1)} %constant.16.clone.refs_4_) | copy-start | bytes 786436
  6.8 0.9 %copy-start.6 = (bf16[4,54,144]{2,1,0:T(8,128)(2,1)S(1)}, bf16[4,54,144]{2,1,0:T(8,128)(2,1)}, u32[]{:S(2)}) copy-start(bf16[4,54,144]{2,1,0:T(8,128)(2,1)} %constant.18.clone.refs_11_) | copy-start | bytes 186628
  7.7 0.9 %copy-start.7 = (bf16[4,72,54]{2,1,0:T(8,128)(2,1)S(1)}, bf16[4,72,54]{2,1,0:T(8,128)(2,1)}, u32[]{:S(2)}) copy-start(bf16[4,72,54]{2,1,0:T(8,128)(2,1)} %constant.19.clone.refs_12_) | copy-start | bytes 93316
  8.6 0.8 %copy-start.8 = (bf16[64,256]{1,0:T(8,128)(2,1)S(1)}, bf16[64,256]{1,0:T(8,128)(2,1)}, u32[]{:S(2)}) copy-start(bf16[64,256]{1,0:T(8,128)(2,1)} %constant.20.clone.refs_13_) | copy-start | bytes 98308
  9.3 0.7 %copy-start.9 = (bf16[64,54]{0,1:T(8,128)(2,1)S(1)}, bf16[64,54]{0,1:T(8,128)(2,1)}, u32[]{:S(2)}) copy-start(bf16[64,54]{0,1:T(8,128)(2,1)} %param.17) | copy-start | bytes 20740
  10.0 0.7 %copy-start.10 = (bf16[54,64]{1,0:T(8,128)(2,1)S(1)}, bf16[54,64]{1,0:T(8,128)(2,1)}, u32[]{:S(2)}) copy-start(bf16[54,64]{1,0:T(8,128)(2,1)} %refs_9_.1) | copy-start | bytes 20740

commit v2 on v1

--- a/solution.py
+++ b/solution.py
@@ -14,13 +14,14 @@
 X_CHIPS = 4
 W = 192
 CH = 64
+BIAS_TAP = 48 + 16 + 12
 ROWS = 8
 F32 = jnp.float32
 BF16 = jnp.bfloat16
 MESH = pl.DeviceIdType.MESH
 
 PACKED = np.concatenate([np.arange(0, 128), np.arange(192, 320), np.arange(128, 192), np.arange(320, 384)])
-OFFSETS = [(i, j) for i in (-1, 0, 1) for j in (-1, 0, 1) if (i, j) != (0, 0)]
+STRIPS = [(1, 1), (1, -1), (-1, 1), (-1, -1), (1, 0), (-1, 0)]
 
 
 def split_halves(table):
@@ -86,13 +87,14 @@
     return jnp.concatenate([real[0], imag[0], third], axis=1)
 
 
-def kernel(n, sections, meas_hbm, maps_hbm, th_hbm, tl_hbm, eh_hbm, el_hbm,
-           samp_ref, first_ref, bias_first_ref, second_ref, bias_second_ref, pick_first_ref, pick_second_ref,
-           repeat_ref, out_ref,
-           meas, maps, th, tl, eh, el, masked, spread, outgoing, gathered, gathered_f, gathered_swap,
-           part, got1, sum1, got2, sum2, got3, weight1, weight2, bias_full, edge_out, edge_in, grid_rows, grid_half,
+def kernel(n, sections, meas_hbm, maps_hbm, samp_hbm, th_hbm, tl_hbm, eh_hbm, el_hbm,
+           first_hbm, bias_first_hbm, second_hbm, bias_second_hbm, pick_first_hbm, pick_second_hbm, repeat_hbm, out_ref,
+           meas, maps, samp_ref, th, tl, eh, el,
+           first_ref, bias_first_ref, second_ref, bias_second_ref, pick_first_ref, pick_second_ref, repeat_ref, masked, spread, outgoing, gathered, gathered_f, gathered_swap,
+           part, got1, sum1, got2, sum2, got3, weight1, weight2, edge_out, edge_in, strip_rows, strip_out, strip_in, grid_rows, grid_half,
            result, load_sem, maps_send, maps_recv, rs1_send, rs1_recv, rs2_send, rs2_recv, rs3_send, rs3_recv,
-           edge_send, edge_recv):
+           edge_send, edge_recv,
+           strip_send, strip_recv):
     coil = lax.axis_index("coil")
     sect = lax.axis_index("sect")
     core = lax.rem(coil, 2)
@@ -104,7 +106,12 @@
     loads = [
         pltpu.make_async_copy(src, dst, load_sem.at[i])
         for i, (src, dst) in enumerate(
-            [(maps_hbm, maps), (meas_hbm, meas), (th_hbm, th), (tl_hbm, tl), (eh_hbm, eh), (el_hbm, el)]
+            [
+                (samp_hbm, samp_ref), (th_hbm, th), (tl_hbm, tl), (meas_hbm, meas), (eh_hbm, eh), (el_hbm, el),
+                (maps_hbm, maps), (first_hbm, first_ref), (bias_first_hbm, bias_first_ref), (second_hbm, second_ref),
+                (bias_second_hbm, bias_second_ref), (pick_first_hbm, pick_first_ref),
+                (pick_second_hbm, pick_second_ref), (repeat_hbm, repeat_ref),
+            ]
         )
     ]
     for load in loads:
@@ -122,27 +129,8 @@
             peer = (lax.rem(coil + dc + n, n), lax.rem(sect + ds + sections, sections))
             pl.semaphore_signal(barrier, inc=1, device_id=peer, device_id_type=MESH)
 
-    loads[0].wait()
-    turned = [pack_rows(maps[s]).T.reshape(n, ROWS, 384) for s in range(2)]
-    outgoing[...] = jnp.concatenate(turned, axis=1).astype(BF16)
-    gathered[coil] = outgoing[coil]
-    pl.semaphore_wait(barrier, n - 1 + 6)
-
-    def maps_copy(d):
-        peer = lax.rem(coil + d, n)
-        return pltpu.make_async_remote_copy(
-            src_ref=outgoing.at[peer], dst_ref=gathered.at[coil], send_sem=maps_send.at[d], recv_sem=maps_recv.at[d],
-            device_id=(peer, sect), device_id_type=MESH,
-        )
-
-    def send_maps(d, carry):
-        maps_copy(d).start()
-        return carry
-
-    lax.fori_loop(1, n, send_maps, 0)
-
-    loads[2].wait()
-    loads[3].wait()
+    for load in loads[:3]:
+        load.wait()
     for s in range(2):
         mask = samp_ref[s:s + 1, :].astype(F32)
         mask = jnp.concatenate([mask, jnp.zeros((1, 64), F32)], axis=1)
@@ -151,9 +139,8 @@
         masked[s, 0] = (th[...].astype(F32) * mask).astype(BF16)
         masked[s, 1] = (tl[...].astype(F32) * mask).astype(BF16)
 
-    loads[1].wait()
-    loads[4].wait()
-    loads[5].wait()
+    for load in loads[3:7]:
+        load.wait()
     copies1 = []
     for s in range(2):
         xh, xl = halves(pack_rows(meas[s]))
@@ -170,12 +157,31 @@
             y_im = by_cos[im] + by_sin[re]
             terms += [m[re] * y_re + m[im] * y_im, m[re] * y_im - m[im] * y_re]
         part[s] = jnp.concatenate(terms, axis=0).T.reshape(n // 2, 2, ROWS, 384)
+        if s == 0:
+            pl.semaphore_wait(barrier, n - 1 + 6)
         copy = pltpu.make_async_remote_copy(
             src_ref=part.at[s, :, 1 - core], dst_ref=got1.at[s], send_sem=rs1_send.at[s], recv_sem=rs1_recv.at[s],
             device_id=(coil + 1 - 2 * core, sect), device_id_type=MESH,
         )
         copy.start()
         copies1.append(copy)
+
+    turned = [pack_rows(maps[s]).T.reshape(n, ROWS, 384) for s in range(2)]
+    outgoing[...] = jnp.concatenate(turned, axis=1).astype(BF16)
+    gathered[coil] = outgoing[coil]
+
+    def maps_copy(d):
+        peer = lax.rem(coil + d, n)
+        return pltpu.make_async_remote_copy(
+            src_ref=outgoing.at[peer], dst_ref=gathered.at[coil], send_sem=maps_send.at[d], recv_sem=maps_recv.at[d],
+            device_id=(peer, sect), device_id_type=MESH,
+        )
+
+    def send_maps(d, carry):
+        maps_copy(d).start()
+        return carry
+
+    lax.fori_loop(1, n, send_maps, 0)
 
     copies2 = []
     for s in range(2):
@@ -215,8 +221,8 @@
             copy.start()
             copies3.append(copy)
 
-    for s in range(4):
-        weight1[64 * s:64 * s + 64] = dot(first_ref[...], pick_first_ref[s], ((0,), (0,))).astype(BF16)
+    for load in loads[7:]:
+        load.wait()
     repeated = dot(second_ref[...], repeat_ref[...]).astype(BF16)
     of_slice = lax.broadcasted_iota(jnp.int32, (72, 256), 1) // 64
     second = jnp.zeros((72, 256), F32)
@@ -227,12 +233,22 @@
     weight2[...] = second.astype(BF16)
     diagonal = lax.broadcasted_iota(jnp.int32, (64, 64), 0) == lax.broadcasted_iota(jnp.int32, (64, 64), 1)
     bias_column = jnp.sum(jnp.where(diagonal, bias_first_ref[...], 0.0), axis=1, keepdims=True)
+    bias_high = bias_column.astype(BF16).astype(F32)
+    bias_rest = bias_column - bias_high
+    bias_middle = bias_rest.astype(BF16).astype(F32)
+    spot = lax.broadcasted_iota(jnp.int32, (64, 144), 1)
+    bias_taps = jnp.where(spot == BIAS_TAP, bias_high, 0.0)
+    bias_taps = jnp.where(spot == BIAS_TAP + 1, bias_middle, bias_taps)
+    bias_taps = jnp.where(spot == BIAS_TAP + 2, bias_rest - bias_middle, bias_taps)
     for s in range(4):
-        bias_full[64 * s:64 * s + 64] = jnp.broadcast_to(bias_column, (64, 256))
-    grid_rows[...] = jnp.zeros_like(grid_rows)
+        block = dot(first_ref[...], pick_first_ref[s], ((0,), (0,)))
+        weight1[64 * s:64 * s + 64] = (block + bias_taps).astype(BF16)
+    place = lax.rem(lax.broadcasted_iota(jnp.int32, (192, 128), 0), 16)
+    for t in range(2):
+        grid_rows[t] = jnp.where(jnp.logical_and(place >= 12, place < 15), 1.0, 0.0)
 
     def wait_maps(d, carry):
-        maps_copy(d).wait()
+        maps_copy(d).wait_recv()
         return carry
 
     lax.fori_loop(1, n, wait_maps, 0)
@@ -254,9 +270,8 @@
     low = lane < 64
     lanes_in = lax.broadcasted_iota(jnp.int32, (72, 256), 1) < W
     row_of_8 = lax.broadcasted_iota(jnp.int32, (ROWS, 256), 0)
-    bias_rows = jnp.where(lax.rem(row_of_8, 2) == 0, bias_second_ref[0], bias_second_ref[1])
+    bias_rows = jnp.where(lax.rem(row_of_8, 2) == 0, bias_second_ref[0:1, 0:1], bias_second_ref[0:1, 1:2])
     image = first_image
-    edge_copies = []
     for turn in range(ITERS):
         damped = []
         for s in range(2):
@@ -280,80 +295,116 @@
             summed = jnp.concatenate([oa, ob, oc], axis=1)
             damped.append(v - STEP * (summed - first_image[s]))
 
-        edge_out[turn] = jnp.concatenate(damped, axis=0).astype(BF16)
-        copies = []
-        for i, (dc, ds) in enumerate(OFFSETS):
+        parts = [unpack(damped[s]) for s in range(2)]
+        for side, top in enumerate((ROWS - 2, 0)):
+            for s in range(2):
+                for q in range(2):
+                    for t in range(2):
+                        for h in range(2):
+                            row = 8 * t + 4 * h + 2 * s + q
+                            strip_rows[side, row:row + 1, :] = parts[s][q][t][top + h:top + h + 1]
+            strip_out[turn, side] = strip_rows[side].astype(BF16)
+        strips = []
+        for i, (dc, ds) in enumerate(STRIPS):
             peer = (lax.rem(coil + dc + n, n), lax.rem(sect + ds + sections, sections))
             copy = pltpu.make_async_remote_copy(
-                src_ref=edge_out.at[turn], dst_ref=edge_in.at[turn, i],
-                send_sem=edge_send.at[turn, i], recv_sem=edge_recv.at[turn, i],
+                src_ref=strip_out.at[turn, 0 if dc > 0 else 1], dst_ref=strip_in.at[turn, i],
+                send_sem=strip_send.at[turn, i], recv_sem=strip_recv.at[turn, i],
                 device_id=peer, device_id_type=MESH,
             )
+            if ds == 0 and i == 4:
+                edge_out[turn] = jnp.concatenate(damped, axis=0).astype(BF16)
+                sides = []
+                for k, step in enumerate((1, -1)):
+                    across = pltpu.make_async_remote_copy(
+                        src_ref=edge_out.at[turn], dst_ref=edge_in.at[turn, k],
+                        send_sem=edge_send.at[turn, k], recv_sem=edge_recv.at[turn, k],
+                        device_id=(coil, lax.rem(sect + step + sections, sections)), device_id_type=MESH,
+                    )
+                    across.start()
+                    sides.append(across)
             copy.start()
-            copies.append(copy)
-        edge_copies += copies
-
-        for dc, ds in [(0, 0)] + [(-i, -j) for i, j in OFFSETS]:
-            if (dc, ds) == (0, 0):
-                blocks = damped
-            else:
-                i = OFFSETS.index((-dc, -ds))
-                copies[i].wait_recv()
-                inside = jnp.logical_and(
-                    jnp.logical_and(coil + dc >= 0, coil + dc < n),
-                    jnp.logical_and(sect + ds >= 0, sect + ds < sections),
-                )
-                block = jnp.where(inside, edge_in[turn, i].astype(F32), 0.0)
-                blocks = [block[0:ROWS], block[ROWS:2 * ROWS]]
+            strips.append(copy)
+
+        def place_slices(values, ds):
             for s in range(2):
-                for q, value in enumerate(unpack(blocks[s])):
-                    k = 2 * (2 + 2 * ds + s) + q
+                for q in range(2):
                     for t in range(2):
-                        if dc == 0:
-                            grid_rows[t, pl.ds(32 + k, ROWS, stride=16), :] = value[t]
-                        elif dc < 0:
-                            grid_rows[t, k:k + 1, :] = value[t][ROWS - 2:ROWS - 1]
-                            grid_rows[t, 16 + k:17 + k, :] = value[t][ROWS - 1:ROWS]
-                        else:
-                            grid_rows[t, 160 + k:161 + k, :] = value[t][0:1]
-                            grid_rows[t, 176 + k:177 + k, :] = value[t][1:2]
-        rows = jnp.concatenate([grid_rows[0], grid_rows[1]], axis=1)
-        grid_half[0] = pltpu.roll(rows, 1, 1).astype(BF16)
-        grid_half[1] = rows.astype(BF16)
-        grid_half[2] = pltpu.roll(rows, 255, 1).astype(BF16)
-
-        sums = [None] * ROWS
-        for r in range(ROWS + 2):
+                        grid_rows[t, pl.ds(32 + 2 * (2 + 2 * ds + s) + q, ROWS, stride=16), :] = values[s][q][t]
+
+        def halve(first, last):
+            rows = jnp.concatenate([grid_rows[0, first:last], grid_rows[1, first:last]], axis=1)
+            grid_half[0, first:last] = pltpu.roll(rows, 1, 1).astype(BF16)
+            grid_half[1, first:last] = rows.astype(BF16)
+            grid_half[2, first:last] = pltpu.roll(rows, 255, 1).astype(BF16)
+
+        def spots_of(r):
             taps = jnp.concatenate([grid_half[e, 16 * r:16 * r + 48, :] for e in range(3)], axis=0)
-            hidden = jnp.maximum(dot(weight1[...], taps) + bias_full[...], 0.0).astype(BF16)
+            hidden = jnp.maximum(dot(weight1[...], taps), 0.0).astype(BF16)
             spots = jnp.where(lanes_in, dot(weight2[...], hidden), 0.0)
             if r == 0:
                 spots = jnp.where(coil > 0, spots, 0.0)
             if r == ROWS + 1:
                 spots = jnp.where(coil < n - 1, spots, 0.0)
-            for a in range(3):
-                if 0 <= r - a < ROWS:
-                    piece = spots[24 * a:24 * a + 24]
-                    sums[r - a] = piece if sums[r - a] is None else sums[r - a] + piece
+            return spots
+
+        place_slices(parts, 0)
+        if turn == 0:
+            for copy in copies1 + copies2 + copies3:
+                copy.wait_send()
+
+            def wait_sent(d, carry):
+                maps_copy(d).wait_send()
+                return carry
+
+            lax.fori_loop(1, n, wait_sent, 0)
+        for k, step in enumerate((1, -1)):
+            sides[k].wait_recv()
+            inside = jnp.logical_and(sect - step >= 0, sect - step < sections)
+            block = jnp.where(inside, edge_in[turn, k].astype(F32), 0.0)
+            place_slices([unpack(block[0:ROWS]), unpack(block[ROWS:2 * ROWS])], -step)
+        halve(32, 160)
+        spots = {r: spots_of(r) for r in range(2, ROWS)}
+
+        for i, (dc, ds) in reversed(list(enumerate(STRIPS))):
+            strips[i].wait_recv()
+            inside = jnp.logical_and(
+                jnp.logical_and(coil - dc >= 0, coil - dc < n),
+                jnp.logical_and(sect - ds >= 0, sect - ds < sections),
+            )
+            block = jnp.where(inside, strip_in[turn, i].astype(F32), 0.0)
+            for t in range(2):
+                for h in range(2):
+                    to = (0 if dc > 0 else 160) + 16 * h + 2 * (2 - 2 * ds)
+                    grid_rows[t, to:to + 4, :] = block[8 * t + 4 * h:8 * t + 4 * h + 4]
+        halve(0, 32)
+        halve(160, 192)
+        for r in (0, 1, ROWS, ROWS + 1):
+            spots[r] = spots_of(r)
+
         for r in range(ROWS):
-            update = pltpu.roll(sums[r][0:8], 1, 1) + sums[r][8:16] + pltpu.roll(sums[r][16:24], 255, 1) + bias_rows
+            taps = spots[r][0:24] + spots[r + 1][24:48] + spots[r + 2][48:72]
+            update = pltpu.roll(taps[0:8], 1, 1) + taps[8:16] + pltpu.roll(taps[16:24], 255, 1) + bias_rows
             for t in range(2):
-                result[t, 8 * r:8 * r + 8, :] = update[:, 128 * t:128 * t + 128]
+                result[t, 4 * r:4 * r + 4, :] = update[0:4, 128 * t:128 * t + 128]
+        for copy in sides + strips:
+            copy.wait_send()
 
         image = []
         for s in range(2):
-            update = [[result[t, pl.ds(2 * s + q, ROWS, stride=8), :] for t in range(2)] for q in range(2)]
+            update = [[result[t, pl.ds(2 * s + q, ROWS, stride=4), :] for t in range(2)] for q in range(2)]
             if turn < ITERS - 1:
                 image.append(damped[s] + pack(*update))
             else:
-                for q, value in enumerate(unpack(damped[s])):
+                for q, value in enumerate(parts[s]):
                     for t in range(2):
-                        result[t, pl.ds(2 * s + q, ROWS, stride=8), :] = value[t] + update[q][t]
-
-    out_ref[:, 0:128] = result[0]
-    out_ref[:, 128:256] = result[1]
-    for copy in copies1 + copies2 + copies3 + edge_copies:
-        copy.wait_send()
+                        result[t, pl.ds(2 * s + q, ROWS, stride=4), :] = value[t] + update[q][t]
+
+    for r in range(ROWS):
+        for s in range(2):
+            rows = slice(4 * r + 2 * s, 4 * r + 2 * s + 2)
+            out_ref[r, s, :, 0:128] = result[0, rows]
+            out_ref[r, s, :, 128:W] = result[1, rows, 0:W - 128]
 
 
 def per_device(n, sections, measured, coil_maps, sampling, conv_first, bias_first, conv_second, bias_second):
@@ -363,21 +414,27 @@
     chips = n // 2
     x_size = min(X_CHIPS, chips // 2)
     z_size = chips // x_size
-    vmem = pl.BlockSpec(memory_space=pltpu.VMEM)
-    hbm = pl.BlockSpec(memory_space=pl.ANY)
     dma = pltpu.SemaphoreType.DMA
     out = pl.pallas_call(
         lambda *refs: kernel(n, sections, *refs),
-        out_shape=jax.ShapeDtypeStruct((8 * ROWS, 256), F32),
-        in_specs=[hbm] * 6 + [vmem] * 4 + [pl.BlockSpec(memory_space=pltpu.SMEM)] + [vmem] * 3,
-        out_specs=vmem,
+        out_shape=pltpu.VMEM((ROWS, 2, 2, W), F32),
+        in_specs=[pl.BlockSpec(memory_space=pl.ANY)] * 14,
+        out_specs=pl.BlockSpec(memory_space=pltpu.VMEM),
         scratch_shapes=[
             pltpu.VMEM((2, 384, height), F32),
             pltpu.VMEM((2, 384, height), F32),
+            pltpu.VMEM((2, W), jnp.int32),
             pltpu.VMEM((384, 384), BF16),
             pltpu.VMEM((384, 384), BF16),
             pltpu.VMEM((height, 2 * height), BF16),
             pltpu.VMEM((height, 2 * height), BF16),
+            pltpu.VMEM((54, CH), BF16),
+            pltpu.VMEM((1, CH), F32),
+            pltpu.VMEM((54, CH), BF16),
+            pltpu.VMEM((1, 2), F32),
+            pltpu.VMEM((4, 54, 144), BF16),
+            pltpu.VMEM((4, 72, 54), BF16),
+            pltpu.VMEM((CH, 256), BF16),
             pltpu.VMEM((2, 2, 384, 384), BF16),
             pltpu.VMEM((2, 2, 384, 384), BF16),
             pltpu.VMEM((n, 2 * ROWS, 384), BF16),
@@ -392,13 +449,15 @@
             pltpu.VMEM((2, z_size - 1, ROWS, 384), F32),
             pltpu.VMEM((256, 144), BF16),
             pltpu.VMEM((72, 256), BF16),
-            pltpu.VMEM((256, 256), F32),
             pltpu.VMEM((ITERS, 2 * ROWS, 384), BF16),
-            pltpu.VMEM((ITERS, 8, 2 * ROWS, 384), BF16),
+            pltpu.VMEM((ITERS, 2, 2 * ROWS, 384), BF16),
+            pltpu.VMEM((2, 16, 128), F32),
+            pltpu.VMEM((ITERS, 2, 16, 128), BF16),
+            pltpu.VMEM((ITERS, 6, 16, 128), BF16),
             pltpu.VMEM((2, 192, 128), F32),
             pltpu.VMEM((3, 192, 256), BF16),
-            pltpu.VMEM((2, 8 * ROWS, 128), F32),
-            dma((6,)),
+            pltpu.VMEM((2, 4 * ROWS, 128), F32),
+            dma((14,)),
             dma((n,)),
             dma((n,)),
             dma((2,)),
@@ -407,18 +466,20 @@
             dma((2, x_size - 1)),
             dma((2, z_size - 1)),
             dma((2, z_size - 1)),
-            dma((ITERS, 8)),
-            dma((ITERS, 8)),
+            dma((ITERS, 2)),
+            dma((ITERS, 2)),
+            dma((ITERS, 6)),
+            dma((ITERS, 6)),
         ],
         compiler_params=pltpu.CompilerParams(
-            collective_id=0, has_side_effects=True, vmem_limit_bytes=40 * 1024 * 1024
+            collective_id=0, has_side_effects=True, vmem_limit_bytes=60 * 1024 * 1024
         ),
         name="reconstruct",
     )(
-        by_columns(measured), by_columns(coil_maps), *consts[:4],
-        sampling, conv_first.T, bias_first.reshape(1, CH), conv_second, bias_second, *consts[4:],
+        by_columns(measured), by_columns(coil_maps), sampling, *consts[:4],
+        conv_first.T, bias_first.reshape(1, CH), conv_second, bias_second.reshape(1, 2), *consts[4:],
     )
-    return out.reshape(ROWS, 8, 256)[:, :4, :W].reshape(ROWS, 2, 2, W)
+    return out
 
 
 def solution(mesh):

time: 60 us -> 43.8 us (0.73)
  local copies, waits for them, and re-layouts: 11.4 us -> 0.62 us
  Pallas kernels: 48.1 us -> 43.1 us
    unnamed x28 -> x1, local copies, waits for them, and re-layouts: 10.7 us -> 0.62 us
    pallas_call x1, Pallas kernels: 48.1 us -> 43.1 us  [per_device(): pl.pallas_call(lambda *refs: kernel(n, sections, *refs), out_shape=pltpu....]
    reshape x1 -> x0, local copies, waits for them, and re-layouts: 0.64 us -> none  [per_device(): return out.reshape(ROWS, 8, 256)[:, :4, :W].reshape(ROWS, 2, 2, W)]
where the time goes in v2:
time: 43.8 us; the launch traced here: 43.7 us
  Pallas kernels  43.1 us (98%)
  local copies, waits for them, and re-layouts  0.62 us (1%)
    pallas_call x1, Pallas kernels, per_device(): pl.pallas_call(lambda *refs: kernel(n, sections, *refs), out_shape=pltpu....  43.1 us

profile of v2, /device:TPU:1, one launch (start us, length us, event | category | flops | bytes accessed | tf_op | source)
XLA Modules:
  0.0 43.7 jit_solution(7067779049982369254)
XLA Ops:
  0.0 43.1 %reconstruct.1 = f32[8,2,2,192]{3,2,1,0:T(2,128)S(1)} custom-call(f32[2,384,256]{2,1,0:T(8,128)} %bitcast.9, f32[2,384,256]{2,1,0:T(8,128)} %bitcast.10, s32[2,192]{1,0:T(2,128)} %refs_2_.1, bf16[384,384]{1,0:T(8,128)(2,1)} %constant.14.clone.refs_3_, bf16[384,384]{1,0:T(8,128)(2,1)} %constant.15.clone.refs_4_, bf16[256,512]{1,0:T(8,128)(2,1)} %constant.16.clone.refs_5_, ...), custom_call_target="tpu_custom_call" | custom-call | tf_op jit(solution)/shard_map/reconstruct/pallas_call | solution.py:418
  43.1 0.6 %copy.16 = f32[8,2,2,192]{3,2,1,0:T(2,128)} copy(f32[8,2,2,192]{3,2,1,0:T(2,128)S(1)} %reconstruct.1) | data formatting | bytes 49152

commit v3 on v2

--- a/solution.py
+++ b/solution.py
@@ -136,17 +136,24 @@
         mask = jnp.concatenate([mask, jnp.zeros((1, 64), F32)], axis=1)
         tail = mask[:, 128:256]
         mask = jnp.concatenate([mask[:, 0:128], mask[:, 0:128], tail + pltpu.roll(tail, 64, 1)], axis=1)
-        masked[s, 0] = (th[...].astype(F32) * mask).astype(BF16)
-        masked[s, 1] = (tl[...].astype(F32) * mask).astype(BF16)
+        high = (th[...].astype(F32) * mask).astype(BF16)
+        masked[s, :, 0:384] = high
+        masked[s, :, 384:768] = (tl[...].astype(F32) * mask).astype(BF16)
+        masked[s, :, 768:1152] = high
 
     for load in loads[3:7]:
         load.wait()
     copies1 = []
+    columns = []
     for s in range(2):
         xh, xl = halves(pack_rows(meas[s]))
-        column = dot(masked[s, 0], xh) + dot(masked[s, 0], xl) + dot(masked[s, 1], xh)
-        zh, zl = halves(column)
-        both = dot(zh, eh[...]) + dot(zl, eh[...]) + dot(zh, el[...])
+        columns.append(dot(masked[s], jnp.concatenate([xh, xh, xl], axis=0)))
+    planes = []
+    for s in range(2):
+        zh, zl = halves(columns[s])
+        planes.append(dot(jnp.concatenate([zh, zl, zh], axis=1), jnp.concatenate([eh[...], eh[...], el[...]], axis=0)))
+    for s in range(2):
+        both = planes[s]
         height = both.shape[1] // 2
         by_cos, by_sin = both[:, :height], both[:, height:]
         m = pack_rows(maps[s])
@@ -199,10 +206,10 @@
 
     for s in range(2):
         last = ((1,), (1,))
-        mh, ml = masked[s, 0], masked[s, 1]
-        high, low = halves(dot(mh, mh, last) + dot(mh, ml, last) + dot(ml, mh, last))
-        spread[s, 0] = high
-        spread[s, 1] = low
+        mh, ml = masked[s, :, 0:384], masked[s, :, 384:768]
+        high, low = halves(dot(masked[s], jnp.concatenate([mh, mh, ml], axis=1), last))
+        spread[s, 0:384] = high
+        spread[s, 384:768] = low
 
     copies3 = []
     for s in range(2):
@@ -274,18 +281,24 @@
     image = first_image
     for turn in range(ITERS):
         damped = []
+        products = []
         for s in range(2):
             v = image[s]
-            va, vb, vc = v[:, 0:128], v[:, 128:256], v[:, 256:384]
+            va, vb, vc = v[None, :, 0:128], v[None, :, 128:256], v[:, 256:384]
             turned_c = pltpu.roll(vc, 64, 1)
             v_re = jnp.where(low, vc, turned_c)[None]
             v_im = jnp.where(low, -turned_c, vc)[None]
             ma, mb, mc = gathered_f[s, :, :, 0:128], gathered_f[s, :, :, 128:256], gathered_f[s, :, :, 256:384]
             ms = gathered_swap[s]
-            va, vb = va[None], vb[None]
             pieces = [ma * va - mb * vb, ma * vb + mb * va, mc * v_re + ms * v_im]
             product = jnp.concatenate([p.reshape(n * ROWS, 128) for p in pieces], axis=1).astype(BF16)
-            back = (dot(product, spread[s, 0]) + dot(product, spread[s, 1])).reshape(n, ROWS, 384)
+            products.append(product)
+        backs = [dot(jnp.concatenate([p, p], axis=1), spread[s]) for s, p in enumerate(products)]
+        for s in range(2):
+            v = image[s]
+            back = backs[s].reshape(n, ROWS, 384)
+            ma, mb, mc = gathered_f[s, :, :, 0:128], gathered_f[s, :, :, 128:256], gathered_f[s, :, :, 256:384]
+            ms = gathered_swap[s]
             qa, qb, qc = back[:, :, 0:128], back[:, :, 128:256], back[:, :, 256:384]
             oa = jnp.sum(ma * qa + mb * qb, axis=0)
             ob = jnp.sum(ma * qb - mb * qa, axis=0)
@@ -338,9 +351,11 @@
             grid_half[1, first:last] = rows.astype(BF16)
             grid_half[2, first:last] = pltpu.roll(rows, 255, 1).astype(BF16)
 
-        def spots_of(r):
+        def hidden_of(r):
             taps = jnp.concatenate([grid_half[e, 16 * r:16 * r + 48, :] for e in range(3)], axis=0)
-            hidden = jnp.maximum(dot(weight1[...], taps), 0.0).astype(BF16)
+            return jnp.maximum(dot(weight1[...], taps), 0.0).astype(BF16)
+
+        def spots_of(r, hidden):
             spots = jnp.where(lanes_in, dot(weight2[...], hidden), 0.0)
             if r == 0:
                 spots = jnp.where(coil > 0, spots, 0.0)
@@ -364,7 +379,8 @@
             block = jnp.where(inside, edge_in[turn, k].astype(F32), 0.0)
             place_slices([unpack(block[0:ROWS]), unpack(block[ROWS:2 * ROWS])], -step)
         halve(32, 160)
-        spots = {r: spots_of(r) for r in range(2, ROWS)}
+        hidden = {r: hidden_of(r) for r in range(2, ROWS)}
+        spots = {r: spots_of(r, hidden[r]) for r in range(2, ROWS)}
 
         for i, (dc, ds) in reversed(list(enumerate(STRIPS))):
             strips[i].wait_recv()
@@ -379,8 +395,9 @@
                     grid_rows[t, to:to + 4, :] = block[8 * t + 4 * h:8 * t + 4 * h + 4]
         halve(0, 32)
         halve(160, 192)
-        for r in (0, 1, ROWS, ROWS + 1):
-            spots[r] = spots_of(r)
+        hidden = {r: hidden_of(r) for r in (0, 1, ROWS, ROWS + 1)}
+        for r in hidden:
+            spots[r] = spots_of(r, hidden[r])
 
         for r in range(ROWS):
             taps = spots[r][0:24] + spots[r + 1][24:48] + spots[r + 2][48:72]
@@ -435,8 +452,8 @@
             pltpu.VMEM((4, 54, 144), BF16),
             pltpu.VMEM((4, 72, 54), BF16),
             pltpu.VMEM((CH, 256), BF16),
-            pltpu.VMEM((2, 2, 384, 384), BF16),
-            pltpu.VMEM((2, 2, 384, 384), BF16),
+            pltpu.VMEM((2, 384, 1152), BF16),
+            pltpu.VMEM((2, 768, 384), BF16),
             pltpu.VMEM((n, 2 * ROWS, 384), BF16),
             pltpu.VMEM((n, 2 * ROWS, 384), BF16),
             pltpu.VMEM((2, n, ROWS, 384), F32),

time: 43.8 us -> 40.7 us (0.929)
  Pallas kernels: 43.1 us -> 39.8 us
    pallas_call x1, Pallas kernels: 43.1 us -> 39.8 us  [per_device(): pl.pallas_call(lambda *refs: kernel(n, sections, *refs), out_shape=pltpu....]
where the time goes in v3:
time: 40.7 us; the launch traced here: 40.4 us
  Pallas kernels  39.8 us (98%)
  local copies, waits for them, and re-layouts  0.62 us (2%)
    pallas_call x1, Pallas kernels, per_device(): pl.pallas_call(lambda *refs: kernel(n, sections, *refs), out_shape=pltpu....  39.8 us

profile of v3, /device:TPU:1, one launch (start us, length us, event | category | flops | bytes accessed | tf_op | source)
XLA Modules:
  0.0 40.4 jit_solution(4496202887913912022)
XLA Ops:
  0.0 39.8 %reconstruct.1 = f32[8,2,2,192]{3,2,1,0:T(2,128)S(1)} custom-call(f32[2,384,256]{2,1,0:T(8,128)} %bitcast.9, f32[2,384,256]{2,1,0:T(8,128)} %bitcast.10, s32[2,192]{1,0:T(2,128)} %refs_2_.1, bf16[384,384]{1,0:T(8,128)(2,1)} %constant.14.clone.refs_3_, bf16[384,384]{1,0:T(8,128)(2,1)} %constant.15.clone.refs_4_, bf16[256,512]{1,0:T(8,128)(2,1)} %constant.16.clone.refs_5_, ...), custom_call_target="tpu_custom_call" | custom-call | tf_op jit(solution)/shard_map/reconstruct/pallas_call | solution.py:435
  39.8 0.6 %copy.16 = f32[8,2,2,192]{3,2,1,0:T(2,128)} copy(f32[8,2,2,192]{3,2,1,0:T(2,128)S(1)} %reconstruct.1) | data formatting | bytes 49152

commit v4 on v3

--- a/solution.py
+++ b/solution.py
@@ -100,8 +100,10 @@
     core = lax.rem(coil, 2)
     x_size = sum1.shape[2]
     z_size = sum1.shape[1]
+    plane = 2 * x_size
+    spot_in_plane = lax.rem(coil, plane)
     x = lax.rem(coil // 2, x_size)
-    z = coil // (2 * x_size)
+    z = coil // plane
 
     loads = [
         pltpu.make_async_copy(src, dst, load_sem.at[i])
@@ -114,7 +116,7 @@
             ]
         )
     ]
-    for load in loads:
+    for load in loads[:7]:
         load.start()
 
     barrier = pltpu.get_barrier_semaphore()
@@ -129,25 +131,23 @@
             peer = (lax.rem(coil + dc + n, n), lax.rem(sect + ds + sections, sections))
             pl.semaphore_signal(barrier, inc=1, device_id=peer, device_id_type=MESH)
 
+    for load in loads[7:]:
+        load.start()
     for load in loads[:3]:
         load.wait()
-    for s in range(2):
-        mask = samp_ref[s:s + 1, :].astype(F32)
-        mask = jnp.concatenate([mask, jnp.zeros((1, 64), F32)], axis=1)
-        tail = mask[:, 128:256]
-        mask = jnp.concatenate([mask[:, 0:128], mask[:, 0:128], tail + pltpu.roll(tail, 64, 1)], axis=1)
-        high = (th[...].astype(F32) * mask).astype(BF16)
-        masked[s, :, 0:384] = high
-        masked[s, :, 384:768] = (tl[...].astype(F32) * mask).astype(BF16)
-        masked[s, :, 768:1152] = high
+    flags = jnp.concatenate([samp_ref[...].astype(F32), jnp.zeros((2, 64), F32)], axis=1)
+    flags = jnp.concatenate([flags, jnp.zeros((6, 256), F32)], axis=0).T
+    table = jnp.concatenate([th[...], tl[...], th[...]], axis=1)
 
     for load in loads[3:7]:
         load.wait()
     copies1 = []
     columns = []
     for s in range(2):
-        xh, xl = halves(pack_rows(meas[s]))
-        columns.append(dot(masked[s], jnp.concatenate([xh, xh, xl], axis=0)))
+        flag = flags[:, s:s + 1]
+        flag = jnp.concatenate([flag[0:128], flag[0:128], flag[128:W], flag[128:W]], axis=0)
+        xh, xl = halves(pack_rows(meas[s]) * flag)
+        columns.append(dot(table, jnp.concatenate([xh, xh, xl], axis=0)))
     planes = []
     for s in range(2):
         zh, zl = halves(columns[s])
@@ -178,7 +178,7 @@
     gathered[coil] = outgoing[coil]
 
     def maps_copy(d):
-        peer = lax.rem(coil + d, n)
+        peer = lax.rem(z + d // plane, z_size) * plane + lax.rem(spot_in_plane + d, plane)
         return pltpu.make_async_remote_copy(
             src_ref=outgoing.at[peer], dst_ref=gathered.at[coil], send_sem=maps_send.at[d], recv_sem=maps_recv.at[d],
             device_id=(peer, sect), device_id_type=MESH,
@@ -188,7 +188,7 @@
         maps_copy(d).start()
         return carry
 
-    lax.fori_loop(1, n, send_maps, 0)
+    lax.fori_loop(plane, n, send_maps, 0)
 
     copies2 = []
     for s in range(2):
@@ -204,6 +204,16 @@
             copy.start()
             copies2.append(copy)
 
+    lax.fori_loop(1, plane, send_maps, 0)
+    for s in range(2):
+        mask = samp_ref[s:s + 1, :].astype(F32)
+        mask = jnp.concatenate([mask, jnp.zeros((1, 64), F32)], axis=1)
+        tail = mask[:, 128:256]
+        mask = jnp.concatenate([mask[:, 0:128], mask[:, 0:128], tail + pltpu.roll(tail, 64, 1)], axis=1)
+        high = (th[...].astype(F32) * mask).astype(BF16)
+        masked[s, :, 0:384] = high
+        masked[s, :, 384:768] = (tl[...].astype(F32) * mask).astype(BF16)
+        masked[s, :, 768:1152] = high
     for s in range(2):
         last = ((1,), (1,))
         mh, ml = masked[s, :, 0:384], masked[s, :, 384:768]

time: 40.7 us -> 40.5 us (level)
  the two profiles are of different devices: /device:TPU:1 before, /device:TPU:32 now
where the time goes in v4:
time: 40.5 us; the launch traced here: 40.4 us
  Pallas kernels  39.8 us (98%)
  local copies, waits for them, and re-layouts  0.62 us (2%)
    pallas_call x1, Pallas kernels, per_device(): pl.pallas_call(lambda *refs: kernel(n, sections, *refs), out_shape=pltpu....  39.8 us

profile of v4, /device:TPU:32, one launch (start us, length us, event | category | flops | bytes accessed | tf_op | source)
XLA Modules:
  0.0 40.4 jit_solution(3304893315154885137)
XLA Ops:
  0.0 39.8 %reconstruct.1 = f32[8,2,2,192]{3,2,1,0:T(2,128)S(1)} custom-call(f32[2,384,256]{2,1,0:T(8,128)} %bitcast.9, f32[2,384,256]{2,1,0:T(8,128)} %bitcast.10, s32[2,192]{1,0:T(2,128)} %refs_2_.1, bf16[384,384]{1,0:T(8,128)(2,1)} %constant.14.clone.refs_3_, bf16[384,384]{1,0:T(8,128)(2,1)} %constant.15.clone.refs_4_, bf16[256,512]{1,0:T(8,128)(2,1)} %constant.16.clone.refs_5_, ...), custom_call_target="tpu_custom_call" | custom-call | tf_op jit(solution)/shard_map/reconstruct/pallas_call | solution.py:445
  39.8 0.6 %copy.16 = f32[8,2,2,192]{3,2,1,0:T(2,128)} copy(f32[8,2,2,192]{3,2,1,0:T(2,128)S(1)} %reconstruct.1) | data formatting | bytes 49152

commit v5 on v4

--- a/solution.py
+++ b/solution.py
@@ -188,7 +188,11 @@
         maps_copy(d).start()
         return carry
 
-    lax.fori_loop(plane, n, send_maps, 0)
+    def send_far(d, carry):
+        maps_copy(plane + lax.rem(d, n - plane)).start()
+        return carry
+
+    lax.fori_loop(plane, n, send_far, 0)
 
     copies2 = []
     for s in range(2):

time: 40.5 us -> 40.1 us (level)
  the two profiles are of different devices: /device:TPU:32 before, /device:TPU:1 now
where the time goes in v5:
time: 40.1 us; the launch traced here: 40 us
  Pallas kernels  39.4 us (98%)
  local copies, waits for them, and re-layouts  0.62 us (2%)
    pallas_call x1, Pallas kernels, per_device(): pl.pallas_call(lambda *refs: kernel(n, sections, *refs), out_shape=pltpu....  39.4 us

profile of v5, /device:TPU:1, one launch (start us, length us, event | category | flops | bytes accessed | tf_op | source)
XLA Modules:
  0.0 40.0 jit_solution(3178220646430937721)
XLA Ops:
  0.0 39.4 %reconstruct.1 = f32[8,2,2,192]{3,2,1,0:T(2,128)S(1)} custom-call(f32[2,384,256]{2,1,0:T(8,128)} %bitcast.9, f32[2,384,256]{2,1,0:T(8,128)} %bitcast.10, s32[2,192]{1,0:T(2,128)} %refs_2_.1, bf16[384,384]{1,0:T(8,128)(2,1)} %constant.14.clone.refs_3_, bf16[384,384]{1,0:T(8,128)(2,1)} %constant.15.clone.refs_4_, bf16[256,512]{1,0:T(8,128)(2,1)} %constant.16.clone.refs_5_, ...), custom_call_target="tpu_custom_call" | custom-call | tf_op jit(solution)/shard_map/reconstruct/pallas_call | solution.py:449
  39.4 0.6 %copy.16 = f32[8,2,2,192]{3,2,1,0:T(2,128)} copy(f32[8,2,2,192]{3,2,1,0:T(2,128)S(1)} %reconstruct.1) | data formatting | bytes 49152

commit v6 on v5

--- a/solution.py
+++ b/solution.py
@@ -194,11 +194,11 @@
 
     lax.fori_loop(plane, n, send_far, 0)
 
-    copies2 = []
+    copies2 = {}
     for s in range(2):
         copies1[s].wait_recv()
         sum1[s] = (part[s, :, core] + got1[s]).reshape(z_size, x_size, ROWS, 384)
-        for d in range(1, x_size):
+        for d in [x_size // 2] + [i for i in range(1, x_size) if i != x_size // 2]:
             to = lax.rem(x + d, x_size)
             copy = pltpu.make_async_remote_copy(
                 src_ref=sum1.at[s, :, to], dst_ref=got2.at[s, d - 1],
@@ -206,7 +206,7 @@
                 device_id=((z * x_size + to) * 2 + core, sect), device_id_type=MESH,
             )
             copy.start()
-            copies2.append(copy)
+            copies2[s, d] = copy
 
     lax.fori_loop(1, plane, send_maps, 0)
     for s in range(2):
@@ -225,14 +225,14 @@
         spread[s, 0:384] = high
         spread[s, 384:768] = low
 
-    copies3 = []
+    copies3 = {}
     for s in range(2):
         total = sum1[s, :, x]
         for d in range(1, x_size):
-            copies2[s * (x_size - 1) + d - 1].wait_recv()
+            copies2[s, d].wait_recv()
             total = total + got2[s, d - 1]
         sum2[s] = total
-        for d in range(1, z_size):
+        for d in [z_size // 2] + [i for i in range(1, z_size) if i != z_size // 2]:
             to = lax.rem(z + d, z_size)
             copy = pltpu.make_async_remote_copy(
                 src_ref=sum2.at[s, to], dst_ref=got3.at[s, d - 1],
@@ -240,7 +240,7 @@
                 device_id=((to * x_size + x) * 2 + core, sect), device_id_type=MESH,
             )
             copy.start()
-            copies3.append(copy)
+            copies3[s, d] = copy
 
     for load in loads[7:]:
         load.wait()
@@ -283,7 +283,7 @@
     for s in range(2):
         total = sum2[s, z]
         for d in range(1, z_size):
-            copies3[s * (z_size - 1) + d - 1].wait_recv()
+            copies3[s, d].wait_recv()
             total = total + got3[s, d - 1]
         first_image.append(total)
 
@@ -379,7 +379,7 @@
 
         place_slices(parts, 0)
         if turn == 0:
-            for copy in copies1 + copies2 + copies3:
+            for copy in copies1 + list(copies2.values()) + list(copies3.values()):
                 copy.wait_send()
 
             def wait_sent(d, carry):

time: 40.1 us -> 40.1 us (level)
  no operation moved by 1% of the time
where the time goes in v6:
time: 40.1 us; the launch traced here: 39.9 us
  Pallas kernels  39.3 us (98%)
  local copies, waits for them, and re-layouts  0.62 us (2%)
    pallas_call x1, Pallas kernels, per_device(): pl.pallas_call(lambda *refs: kernel(n, sections, *refs), out_shape=pltpu....  39.3 us

profile of v6, /device:TPU:1, one launch (start us, length us, event | category | flops | bytes accessed | tf_op | source)
XLA Modules:
  0.0 39.9 jit_solution(5999650403361246961)
XLA Ops:
  0.0 39.3 %reconstruct.1 = f32[8,2,2,192]{3,2,1,0:T(2,128)S(1)} custom-call(f32[2,384,256]{2,1,0:T(8,128)} %bitcast.9, f32[2,384,256]{2,1,0:T(8,128)} %bitcast.10, s32[2,192]{1,0:T(2,128)} %refs_2_.1, bf16[384,384]{1,0:T(8,128)(2,1)} %constant.14.clone.refs_3_, bf16[384,384]{1,0:T(8,128)(2,1)} %constant.15.clone.refs_4_, bf16[256,512]{1,0:T(8,128)(2,1)} %constant.16.clone.refs_5_, ...), custom_call_target="tpu_custom_call" | custom-call | tf_op jit(solution)/shard_map/reconstruct/pallas_call | solution.py:449
  39.3 0.6 %copy.16 = f32[8,2,2,192]{3,2,1,0:T(2,128)} copy(f32[8,2,2,192]{3,2,1,0:T(2,128)S(1)} %reconstruct.1) | data formatting | bytes 49152
